TPU v7x, 32 devices: a whole 2x2x4 slice. The times are simulated.
32 devices in a mesh: sec: 4 (over y, x), feat: 2 (over core), row: 4 (over z).
Axes of the slice: x: 2, y: 2, z: 4, core: 2. Of those that a mesh axis runs over, the one named last changes fastest.
Arguments:
- inputs: bfloat16 [4, 1024, 2304], P('sec', 'row', 'feat'), may hold values from -6 to 6
- enc_weight: bfloat16 [4, 2304, 16384], P('sec', None, 'feat'), may hold values from -0.125 to 0.125
- enc_bias: float32 [4, 16384], P('sec', 'feat'), may hold values from -0.5 to 0.5
- dec_weight: bfloat16 [4, 4, 16384, 2304], P('sec', None, 'feat', 'row'), may hold values from -0.046875 to 0.046875
- dec_bias: float32 [4, 2304], P('sec', 'row'), may hold values from -3 to 3
Outputs:
- recon: bfloat16 [4, 1024, 2304], P('sec', 'feat', 'row')
All inputs are finite; a program needn't handle non-finite values.
Results may differ from a plain program's by a relative error of at most 0.0047.
Values may be sent and summed in bfloat16 or wider, within the bound.
A program may use at most 256 MiB of HBM per device.

v0:
```python
import jax
import jax.numpy as jnp
from jax import lax
from jax.sharding import PartitionSpec as P


def per_device(inputs, enc_weight, enc_bias, dec_weight, dec_bias):
    encoder = enc_weight[0]
    decoders = dec_weight[0]
    target = lax.axis_index("sec")
    hidden = jnp.dot(
        lax.all_gather(inputs[0], "feat", axis=1, tiled=True),
        encoder,
        preferred_element_type=jnp.float32,
    )
    features = jnp.maximum(hidden + enc_bias[0], 0.0).astype(jnp.bfloat16)
    every_row = lax.all_gather(features, "row", axis=0, tiled=True)

    def decode_one(totals, block, source):
        weight = lax.dynamic_index_in_dim(decoders, source, 0, keepdims=False)
        return totals + jnp.dot(block, weight, preferred_element_type=jnp.float32)

    empty_dec = jnp.zeros((every_row.shape[0], decoders.shape[2]), jnp.float32)
    totals = empty_dec
    piece = lax.all_gather(every_row[None], "sec", axis=0, tiled=True)
    start = jnp.int32(0)
    for offset in range(piece.shape[0]):
        source = start + offset
        totals = lax.cond(
            source <= target,
            lambda acc: decode_one(acc, piece[offset], source),
            lambda acc: acc,
            totals,
        )
    summed = lax.psum_scatter(totals, "feat", scatter_dimension=0, tiled=True)
    return (summed + dec_bias[0]).astype(jnp.bfloat16)[None]


def solution(mesh):
    in_specs = (
        P("sec", "row", "feat"),
        P("sec", None, "feat"),
        P("sec", "feat"),
        P("sec", None, "feat", "row"),
        P("sec", "row"),
    )
    out_specs = P("sec", "feat", "row")
    return jax.shard_map(
        per_device, mesh=mesh, in_specs=in_specs, out_specs=out_specs, check_vma=False
    )
```

profile of v0, /device:TPU:0, one launch (start us, length us, event | category | flops | bytes accessed | tf_op | source)
XLA Modules:
  0.0 984.2 jit_solution(1859742515051008663)
XLA Ops:
  6.5 0.0 all-gather.8.cloned.1.call-start
  6.5 0.7 all-gather.8.cloned.1.call-update
  7.3 0.0 all-gather.6.cloned.1.call-start
  7.3 13.6 %all-gather.8.cloned.1.call-done = bf16[1,256,2304]{2,1,0:T(8,128)(2,1)} async-done(((bf16[1,256,1152]{2,1,0:T(8,128)(2,1)}), bf16[1,256,2304]{2,1,0:T(8,128)(2,1)}) %all-gather.8.cloned.1.call-update) | async-done | bytes 1179664 | tf_op jit(solution)/shard_map/all_gather | solution.py:12
  20.9 18.5 %fusion.43 = bf16[256,8192]{1,0:T(8,128)(2,1)} fusion(bf16[1,2304,8192]{2,1,0:T(8,128)(2,1)} %param.14, f32[8192]{0:T(1024)} %bitcast.57, bf16[1,256,2304]{2,1,0:T(8,128)(2,1)} %all-gather.8.cloned.1.call-done), kind=kOutput, calls=%fused_computation.27 | convolution fusion | flops 9669967872 | bytes 43155456 | tf_op jit(solution)/shard_map/dot_general | solution.py:11
  39.3 0.0 all-gather.6.cloned.1.call-update
  39.3 0.0 all-gather.10.cloned.1.call-start
  39.4 288.1 %all-gather.6.cloned.1.call-done = bf16[1024,8192]{1,0:T(8,128)(2,1)} async-done(((bf16[256,8192]{1,0:T(8,128)(2,1)}), bf16[1024,8192]{1,0:T(8,128)(2,1)}) %all-gather.6.cloned.1.call-update) | async-done | bytes 16777232 | tf_op jit(solution)/shard_map/all_gather | solution.py:17
  327.4 0.0 all-gather.10.cloned.1.call-update
  327.5 0.0 reduce-scatter.2.cloned.1.call-start
  327.5 51.6 %copy.6 = bf16[1,4,8192,576]{3,2,1,0:T(8,128)(2,1)} copy(bf16[1,4,8192,576]{2,3,1,0:T(8,128)(2,1)} %param.16) | data formatting | bytes 75497472 | tf_op args[3]
  379.1 525.2 %all-gather.10.cloned.1.call-done = bf16[4096,8192]{1,0:T(8,128)(2,1)} async-done(((bf16[1024,8192]{1,0:T(8,128)(2,1)}), bf16[4096,8192]{1,0:T(8,128)(2,1)}) %all-gather.10.cloned.1.call-update) | async-done | bytes 67108880 | tf_op jit(solution)/shard_map/all_gather | solution.py:25
  904.3 14.5 %conditional.4 = (f32[1024,576]{0,1:T(8,128)S(1)}) conditional(s32[]{:T(128)} %convert_element_type.21, () %tuple.29, (bf16[4,1024,8192]{2,1,0:T(8,128)(2,1)}, bf16[4,8192,576]{2,1,0:T(8,128)(2,1)}) %tuple.50), branch_computations={%region_0.0_spmd, %region_1.2_spmd} | conditional | flops 9663676416 | bytes 29622280 | solution.py:29
  904.3 14.5 %fusion = f32[1024,576]{0,1:T(8,128)S(1)} fusion(bf16[4,1024,8192]{2,1,0:T(8,128)(2,1)} %get-tuple-element.42, bf16[4,8192,576]{2,1,0:T(8,128)(2,1)} %get-tuple-element.43), kind=kOutput, calls=%fused_computation | convolution fusion | flops 9663676416 | bytes 29622272 | tf_op jit(solution)/shard_map/cond/branch_1_fun/dot_general | solution.py:21
  918.8 0.2 conditional.6
  919.0 0.0 copy-start.1
  919.1 0.0 copy-start
  919.1 1.4 copy-done
  920.5 0.0 reduce-scatter.2.cloned.1.call-update
  920.5 0.0 copy-done.1
  920.6 54.8 %reduce-scatter.2.cloned.1.call-done = f32[512,576]{0,1:T(8,128)} async-done(((f32[1024,576]{0,1:T(8,128)}), f32[512,576]{0,1:T(8,128)}) %reduce-scatter.2.cloned.1.call-update) | async-done | bytes 1179664 | tf_op jit(solution)/shard_map/reduce_scatter | solution.py:35
  975.4 2.2 fusion.47
  (3 shorter events, 0.0 us)
Async XLA Ops:
  6.5 14.3 %all-gather.8.cloned.1.call-start = ((), (), s32[]{:S(2)}) async-start(), calls=%async_computation.3 | async-start | bytes 1769472 | tf_op jit(solution)/shard_map/all_gather | solution.py:12
  7.3 320.2 %all-gather.6.cloned.1.call-start = ((), (), s32[]{:S(2)}) async-start(), calls=%async_computation.1 | async-start | bytes 20971520 | tf_op jit(solution)/shard_map/all_gather | solution.py:17
  39.3 865.0 %all-gather.10.cloned.1.call-start = ((), (), s32[]{:S(2)}) async-start(), calls=%async_computation.4 | async-start | bytes 83886080 | tf_op jit(solution)/shard_map/all_gather | solution.py:25
  327.5 647.9 %reduce-scatter.2.cloned.1.call-start = ((), (), s32[]{:S(2)}) async-start(), calls=%async_computation.2 | async-start | bytes 3538944 | tf_op jit(solution)/shard_map/reduce_scatter | solution.py:35
  919.0 1.5 copy-start.1
  919.1 1.4 copy-start
Sparse Core Ops, SparseCore 0:
  8.9 11.9 all-gather.7
  39.5 287.9 all-gather.5
  329.3 574.9 all-gather.9
  920.6 54.6 reduce-scatter.1
where the time goes:
time: 986 us; the launch traced here: 984 us
  waiting for transfers between devices  882 us (89%)
  local copies, waits for them, and re-layouts  53.1 us (5%)
  matrix products  32.9 us (3%)
  between operations  13.2 us (1%)
    all_gather x1, waiting for transfers between devices, per_device(): piece = lax.all_gather(every_row[None], 'sec', axis=0, tiled=True)  525 us
    all_gather x1, waiting for transfers between devices, per_device(): every_row = lax.all_gather(features, 'row', axis=0, tiled=True)  288 us
    reduce_scatter x1, waiting for transfers between devices, per_device(): summed = lax.psum_scatter(totals, 'feat', scatter_dimension=0, tiled=True)  54.8 us
    unnamed x5, local copies, waits for them, and re-layouts  53.1 us
  transfers between devices with their start and end apart: 4, of which 4 were waited for; matrix products, arithmetic and copies ran while one was open for 5% of the time, Pallas kernels for 0%

commit v1 on v0

v1 whole, which is shorter than its diff:
```python
import jax
import jax.numpy as jnp
from jax import lax
from jax.sharding import PartitionSpec as P


def pairs_of(sections):
    step = 1
    while step < sections:
        step *= 2
    rounds = []
    for flip in range(1, step):
        pairs = [(s, s ^ flip) for s in range(sections) if s < (s ^ flip) < sections]
        rounds.append((flip, pairs))
    return rounds


def gather_feat(block, shards):
    if shards != 2:
        return lax.all_gather(block, "feat", axis=1, tiled=True)
    other = lax.ppermute(block, "feat", [(0, 1), (1, 0)])
    first = lax.axis_index("feat") == 0
    return jnp.where(
        first,
        jnp.concatenate([block, other], axis=1),
        jnp.concatenate([other, block], axis=1),
    )


def scatter_sum_feat(total, shards):
    if shards != 2:
        return lax.psum_scatter(total, "feat", scatter_dimension=0, tiled=True)
    half = total.shape[0] // 2
    me = lax.axis_index("feat")
    give = lax.dynamic_slice_in_dim(total, (1 - me) * half, half, 0)
    keep = lax.dynamic_slice_in_dim(total, me * half, half, 0)
    return keep + lax.ppermute(give, "feat", [(0, 1), (1, 0)])


def dot(a, b):
    return jnp.dot(a, b, preferred_element_type=jnp.float32)


def per_device(sections, shards, inputs, enc_weight, enc_bias, dec_weight, dec_bias):
    encoder, bias, decoders = enc_weight[0], enc_bias[0], dec_weight[0]
    depth = encoder.shape[1]
    me = lax.axis_index("sec")
    rounds = pairs_of(sections)
    end_z = depth * 7 // 32
    end_a = depth * 13 // 32

    def encode(rows, low, high):
        hidden = dot(rows, encoder[:, low:high])
        return jnp.maximum(hidden + bias[low:high], 0.0).astype(jnp.bfloat16)

    def decoder(source, low, high):
        return lax.dynamic_slice(
            decoders, (source, low, 0), (1, high - low, decoders.shape[2])
        )[0]

    lent = []
    for flip, pairs in reversed(rounds):
        mine = decoder(jnp.minimum(me ^ flip, sections - 1), end_a, depth)
        lent.append(lax.ppermute(mine, "sec", [(hi, lo) for lo, hi in pairs]))

    rows_z = encode(gather_feat(inputs[0], shards), 0, end_z)
    near = [lax.ppermute(rows_z, "sec", pairs) for _, pairs in reversed(rounds)]
    every = gather_feat(lax.all_gather(inputs[0], "row", axis=0, tiled=True), shards)
    feats_a = encode(every, end_z, end_a)
    direct = [lax.ppermute(feats_a, "sec", pairs) for _, pairs in reversed(rounds)]
    gathered = [lax.all_gather(block, "row", axis=0, tiled=True) for block in near]
    feats_z = encode(every, 0, end_z)
    feats_w = encode(every, end_a, depth)

    total = dot(feats_z, decoder(me, 0, end_z))
    total += dot(feats_a, decoder(me, end_z, end_a))
    total += dot(feats_w, decoder(me, end_a, depth))
    returned = 0.0
    for i, (flip, pairs) in enumerate(reversed(rounds)):
        source = jnp.minimum(me ^ flip, sections - 1)
        part = scatter_sum_feat(dot(feats_w, lent[i]), shards)
        back = lax.ppermute(part.astype(jnp.bfloat16), "sec", pairs)
        returned = returned + back.astype(jnp.float32)
        total += dot(gathered[i], decoder(source, 0, end_z))
        total += dot(direct[i], decoder(source, end_z, end_a))
    summed = scatter_sum_feat(total, shards) + returned
    return (summed + dec_bias[0]).astype(jnp.bfloat16)[None]


def solution(mesh):
    sections, shards = mesh.shape["sec"], mesh.shape["feat"]
    in_specs = (
        P("sec", "row", "feat"),
        P("sec", None, "feat"),
        P("sec", "feat"),
        P("sec", None, "feat", "row"),
        P("sec", "row"),
    )
    out_specs = P("sec", "feat", "row")

    def per_shard(*arrays):
        return per_device(sections, shards, *arrays)

    return jax.shard_map(
        per_shard, mesh=mesh, in_specs=in_specs, out_specs=out_specs, check_vma=False
    )
```

time: 986 us -> 449 us (0.46)
  waiting for transfers between devices: 882 us -> 180 us
  matrix products: 32.9 us -> 149 us
  starting transfers between devices: 0.12 us -> 71.6 us
  local copies, waits for them, and re-layouts: 53.1 us -> 27.5 us
    all_gather x3 -> x4, waiting for transfers between devices: 827 us -> 0.02 us  [the longest x1 0.02 us: per_device(): lax.all_gather(inputs[0], 'row', axis=0, tiled=True)]
    ppermute x0 -> x18, waiting for transfers between devices: none -> 179 us  [the longest x3 117 us: per_device(): lent.append(lax.ppermute(mine, 'sec', [(hi, lo) for lo, hi in pairs]))]
    dot_general x2 -> x15, matrix products: 32.9 us -> 149 us  [dot(): return jnp.dot(a, b, preferred_element_type=jnp.float32)]
    ppermute x0 -> x18, starting transfers between devices: none -> 71.4 us  [the longest x3 33.1 us: per_device(): back = lax.ppermute(part.astype(jnp.bfloat16), 'sec', pairs)]
    reduce_scatter x1 -> x0, waiting for transfers between devices: 54.8 us -> none  [per_device(): summed = lax.psum_scatter(totals, 'feat', scatter_dimension=0, tiled=True)]
    unnamed x5 -> x42, local copies, waits for them, and re-layouts: 53.1 us -> 9.26 us
    squeeze x0 -> x1, local copies, waits for them, and re-layouts: none -> 12.9 us  [decoder(): lax.dynamic_slice(decoders, (source, low, 0), (1, high - low, decoders.sh...]
  transfers between devices with their start and end apart: 4 -> 22, of which waited for: 4 -> 9; matrix products, arithmetic and copies ran while one was open for 5% -> 38% of each run, Pallas kernels for 0% -> 0%
where the time goes in v1:
time: 449 us; the launch traced here: 448 us
  waiting for transfers between devices  180 us (40%)
  matrix products  149 us (33%)
  starting transfers between devices  71.6 us (16%)
  local copies, waits for them, and re-layouts  27.5 us (6%)
  between operations  13.6 us (3%)
  other arithmetic  7.03 us (2%)
    dot_general x15, matrix products, dot(): return jnp.dot(a, b, preferred_element_type=jnp.float32)  149 us
    ppermute x3, waiting for transfers between devices, per_device(): lent.append(lax.ppermute(mine, 'sec', [(hi, lo) for lo, hi in pairs]))  117 us
    ppermute x3, waiting for transfers between devices, per_device(): near = [lax.ppermute(rows_z, 'sec', pairs) for _, pairs in reversed(rounds)]  42.4 us
    ppermute x3, starting transfers between devices, per_device(): back = lax.ppermute(part.astype(jnp.bfloat16), 'sec', pairs)  33.1 us
    ppermute x3, starting transfers between devices, per_device(): lax.ppermute(feats_a, 'sec', pairs)  18.3 us
    ppermute x3, waiting for transfers between devices, per_device(): back = lax.ppermute(part.astype(jnp.bfloat16), 'sec', pairs)  18.1 us
    ppermute x3, starting transfers between devices, per_device(): near = [lax.ppermute(rows_z, 'sec', pairs) for _, pairs in reversed(rounds)]  14.9 us
    squeeze x1, local copies, waits for them, and re-layouts, decoder(): lax.dynamic_slice(decoders, (source, low, 0), (1, high - low, decoders.sh...  12.9 us
  transfers between devices with their start and end apart: 22, of which 9 were waited for; matrix products, arithmetic and copies ran while one was open for 38% of the time, Pallas kernels for 0%

profile of v1, /device:TPU:0, one launch (start us, length us, event | category | flops | bytes accessed | tf_op | source)
XLA Modules:
  0.0 448.2 jit_solution(5137362276891531185)
XLA Ops:
  6.5 0.7 all-gather.12.cloned.1.call-update
  7.3 0.5 collective-permute-start.1
  7.8 0.7 slice_reduce_fusion.1
  8.5 1.1 collective-permute-done.1
  9.7 6.1 %fusion.23 = bf16[256,1792]{1,0:T(8,128)(2,1)S(1)} fusion(bf16[2304,8192]{1,0:T(8,128)(2,1)} %bitcast.56, bf16[256,1152]{1,0:T(8,128)(2,1)S(1)} %collective-permute-done.1, bf16[256,1152]{1,0:T(8,128)(2,1)} %bitcast.55, pred[]{:T(512)S(6)} %eq.4, f32[1792]{0:T(1024)S(1)} %slice_reduce_fusion.1), kind=kOutput, calls=%fused_computation.20 | convolution fusion | flops 2120613888 | bytes 10361857 | tf_op jit(solution)/shard_map/dot_general | solution.py:41
  15.8 4.8 %collective-permute-start.6 = (bf16[256,1792]{1,0:T(8,128)(2,1)S(1)}, bf16[256,1792]{1,0:T(8,128)(2,1)S(1)}, u32[]{:S(2)}, u32[]{:S(2)}) collective-permute-start(bf16[256,1792]{1,0:T(8,128)(2,1)S(1)} %fusion.23), channel_id=1, source_target_pairs={{0,8},{16,24},{1,9},{17,25},{2,10},{18,26},{3,11},{19,27},{4,12},{... | collective-permute-start | bytes 2752520 | tf_op jit(solution)/shard_map/ppermute | solution.py:67
  20.6 19.8 %collective-permute-done.6 = bf16[256,1792]{1,0:T(8,128)(2,1)S(1)} collective-permute-done((bf16[256,1792]{1,0:T(8,128)(2,1)S(1)}, bf16[256,1792]{1,0:T(8,128)(2,1)S(1)}, u32[]{:S(2)}, u32[]{:S(2)}) %collective-permute-start.6) | collective-permute-done | bytes 917536 | tf_op jit(solution)/shard_map/ppermute | solution.py:67
  40.4 0.9 copy-done.11
  41.4 0.0 all-gather.8.cloned.1.call-start
  41.4 3.5 collective-permute-start.4
  44.9 19.0 %collective-permute-done.4 = bf16[256,1792]{1,0:T(8,128)(2,1)S(1)} collective-permute-done((bf16[256,1792]{1,0:T(8,128)(2,1)S(1)}, bf16[256,1792]{1,0:T(8,128)(2,1)S(1)}, u32[]{:S(2)}, u32[]{:S(2)}) %collective-permute-start.4) | collective-permute-done | bytes 917536 | tf_op jit(solution)/shard_map/ppermute | solution.py:67
  63.9 0.9 copy-done.12
  64.9 0.0 all-gather.6.cloned.1.call-start
  65.0 0.1 collective-permute-start
  65.1 6.6 %collective-permute-start.2 = (bf16[256,1792]{1,0:T(8,128)(2,1)}, bf16[256,1792]{1,0:T(8,128)(2,1)S(1)}, u32[]{:S(2)}, u32[]{:S(2)}) collective-permute-start(bf16[256,1792]{1,0:T(8,128)(2,1)} %copy-done.17), channel_id=1, source_target_pairs={{0,24},{8,16},{1,25},{9,17},{2,26},{10,18},{3,27},{11,19},{4,28},{... | collective-permute-start | bytes 2752520 | tf_op jit(solution)/shard_map/ppermute | solution.py:67
  71.7 12.9 %dynamic-slice_bitcast_fusion.2 = (bf16[4864,576]{0,1:T(8,128)(2,1)}, bf16[4864,576]{0,1:T(8,128)(2,1)}, bf16[4864,576]{0,1:T(8,128)(2,1)}) fusion(bf16[1,4,8192,576]{2,3,1,0:T(8,128)(2,1)} %param.8, s32[]{:T(128)S(6)} %select_n.53, s32[]{:T(128)S(6)} %select_n.55, s32[]{:T(128)S(6)} %select_n.54), kind=kLoop, calls=%fused_computation.15 | loop fusion | bytes 33619980 | tf_op jit(solution)/shard_map/squeeze | solution.py:57
  84.6 1.3 collective-permute-start.9
  85.9 1.3 collective-permute-start.15
  87.2 1.3 collective-permute-start.12
  88.5 0.1 slice_reduce_fusion
  88.6 3.6 collective-permute-done.2
  92.2 1.0 copy-done.13
  93.2 12.7 %maximum_convert_fusion.2 = bf16[1024,1536]{1,0:T(8,128)(2,1)} fusion(bf16[2304,8192]{1,0:T(8,128)(2,1)} %bitcast.57, f32[1536]{0:T(1024)S(1)} %slice_reduce_fusion.2, bf16[1024,1152]{1,0:T(8,128)(2,1)} %collective-permute-done, bf16[1024,1152]{1,0:T(8,128)(2,1)S(1)} %bitcast.61, pred[]{:T(512)S(6)} %eq.4), kind=kOutput, calls=%fused_computation.10 | convolution fusion | flops 7273709568 | bytes 14948353 | tf_op jit(solution)/shard_map/dot_general | solution.py:41
  105.9 5.0 %collective-permute-start.7 = (bf16[1024,1536]{1,0:T(8,128)(2,1)}, bf16[1024,1536]{1,0:T(8,128)(2,1)}, u32[]{:S(2)}, u32[]{:S(2)}) collective-permute-start(bf16[1024,1536]{1,0:T(8,128)(2,1)} %maximum_convert_fusion.2), channel_id=1, source_target_pairs={{0,8},{16,24},{1,9},{17,25},{2,10},{18,26},{3,11},{19,27},{4,12},{... | collective-permute-start | bytes 9437192 | tf_op jit(solution)/shard_map/ppermute | solution.py:70
  110.9 10.2 %collective-permute-start.5 = (bf16[1024,1536]{1,0:T(8,128)(2,1)}, bf16[1024,1536]{1,0:T(8,128)(2,1)}, u32[]{:S(2)}, u32[]{:S(2)}) collective-permute-start(bf16[1024,1536]{1,0:T(8,128)(2,1)} %maximum_convert_fusion.2), channel_id=1, source_target_pairs={{0,16},{8,24},{1,17},{9,25},{2,18},{10,26},{3,19},{11,27},{4,20},{... | collective-permute-start | bytes 9437192 | tf_op jit(solution)/shard_map/ppermute | solution.py:70
  121.1 32.5 %maximum_convert_fusion = bf16[1024,4864]{1,0:T(8,128)(2,1)} fusion(bf16[2304,8192]{1,0:T(8,128)(2,1)} %bitcast.58, f32[4864]{0:T(1024)S(1)} %slice_reduce_fusion, bf16[1024,1152]{1,0:T(8,128)(2,1)} %collective-permute-done, bf16[1024,1152]{1,0:T(8,128)(2,1)S(1)} %bitcast.62, pred[]{:T(512)S(6)} %eq.4), kind=kOutput, calls=%fused_computation.2 | convolution fusion | flops 22987407360 | bytes 37112832 | tf_op jit(solution)/shard_map/dot_general | solution.py:41
  153.7 57.7 %collective-permute-done.9 = bf16[4864,576]{0,1:T(8,128)(2,1)} collective-permute-done((bf16[4864,576]{0,1:T(8,128)(2,1)}, bf16[4864,576]{0,1:T(8,128)(2,1)}, u32[]{:S(2)}, u32[]{:S(2)}) %collective-permute-start.9) | collective-permute-done | bytes 5603360 | tf_op jit(solution)/shard_map/ppermute | solution.py:64
  211.3 3.1 collective-permute-start.3
  214.4 10.7 %fusion.77 = f32[1024,576]{0,1:T(8,128)S(1)} fusion(bf16[1024,4864]{1,0:T(8,128)(2,1)} %maximum_convert_fusion, bf16[4864,576]{0,1:T(8,128)(2,1)} %collective-permute-done.9), kind=kOutput, calls=%fused_computation.81 | convolution fusion | flops 5737807872 | bytes 17924096 | tf_op jit(solution)/shard_map/dot_general | solution.py:41
  225.2 1.4 copy-done.5
  226.6 1.1 constant_dynamic-slice_fusion.2
  227.7 18.5 %fusion.32 = f32[1024,576]{0,1:T(8,128)} fusion(bf16[1,4,8192,576]{2,3,1,0:T(8,128)(2,1)} %param.8, s32[]{:T(128)S(6)} %select_n.50, bf16[2304,8192]{1,0:T(8,128)(2,1)} %bitcast.59, f32[1792]{0:T(1024)S(1)} %slice_reduce_fusion.1, bf16[1024,1152]{1,0:T(8,128)(2,1)} %collective-permute-done, bf16[1024,1152]{1,0:T(8,128)(2,1)S(1)} %bitcast.63, pred[]{:T(512)S(6)} %eq.4), kind=kOutput, calls=%fused_computation.28 | convolution fusion | flops 10596384768 | bytes 17406980 | tf_op jit(solution)/shard_map/dot_general | solution.py:41
  246.3 10.4 %fusion.79 = f32[1024,576]{0,1:T(8,128)S(1)} fusion(bf16[1024,4864]{1,0:T(8,128)(2,1)} %maximum_convert_fusion, bf16[4864,576]{0,1:T(8,128)(2,1)} %collective-permute-done.15), kind=kOutput, calls=%fused_computation.83 | convolution fusion | flops 5737807872 | bytes 17924096 | tf_op jit(solution)/shard_map/dot_general | solution.py:41
  256.7 1.4 copy-done.7
  258.1 1.1 constant_dynamic-slice_fusion
  259.2 12.0 %fusion.10 = f32[1024,576]{0,1:T(8,128)} fusion(bf16[1024,4864]{1,0:T(8,128)(2,1)} %maximum_convert_fusion, bf16[1,4,8192,576]{2,3,1,0:T(8,128)(2,1)} %param.8, s32[]{:T(128)S(6)} %select_n.50), kind=kOutput, calls=%fused_computation.11 | convolution fusion | flops 5737807872 | bytes 17924100 | tf_op jit(solution)/shard_map/dot_general | solution.py:41
  271.3 59.4 %collective-permute-done.12 = bf16[4864,576]{0,1:T(8,128)(2,1)} collective-permute-done((bf16[4864,576]{0,1:T(8,128)(2,1)}, bf16[4864,576]{0,1:T(8,128)(2,1)}, u32[]{:S(2)}, u32[]{:S(2)}) %collective-permute-start.12) | collective-permute-done | bytes 5603360 | tf_op jit(solution)/shard_map/ppermute | solution.py:64
  330.7 0.0 collective-permute-start.16
  330.7 8.2 %fusion.78 = f32[1024,576]{0,1:T(8,128)S(1)} fusion(bf16[1024,4864]{1,0:T(8,128)(2,1)S(1)} %bitcast.65, bf16[4864,576]{0,1:T(8,128)(2,1)} %collective-permute-done.12), kind=kOutput, calls=%fused_computation.82 | convolution fusion | flops 5737807872 | bytes 17924096 | tf_op jit(solution)/shard_map/dot_general | solution.py:41
  338.9 1.4 copy-done.9
  340.4 1.2 constant_dynamic-slice_fusion.1
  341.5 5.9 %fusion.44 = f32[1024,576]{0,1:T(8,128)} fusion(bf16[1024,1536]{1,0:T(8,128)(2,1)} %maximum_convert_fusion.2, bf16[1,4,8192,576]{2,3,1,0:T(8,128)(2,1)} %param.8, s32[]{:T(128)S(6)} %select_n.50), kind=kOutput, calls=%fused_computation.40 | convolution fusion | flops 1811939328 | bytes 7274500 | tf_op jit(solution)/shard_map/dot_general | solution.py:41
  347.5 6.4 %fusion.26 = f32[1024,576]{0,1:T(8,128)} fusion(bf16[1024,1792]{1,0:T(8,128)(2,1)} %all-gather.10.cloned.1.call-done, bf16[1,4,8192,576]{2,3,1,0:T(8,128)(2,1)} %param.8, s32[]{:T(128)S(6)} %select_n.55), kind=kOutput, calls=%fused_computation.22 | convolution fusion | flops 2113929216 | bytes 8093700 | tf_op jit(solution)/shard_map/dot_general | solution.py:41
  353.9 6.4 %fusion.28 = f32[1024,576]{0,1:T(8,128)} fusion(bf16[1024,1792]{1,0:T(8,128)(2,1)} %all-gather.8.cloned.1.call-done, bf16[1,4,8192,576]{2,3,1,0:T(8,128)(2,1)} %param.8, s32[]{:T(128)S(6)} %select_n.54), kind=kOutput, calls=%fused_computation.24 | convolution fusion | flops 2113929216 | bytes 8093700 | tf_op jit(solution)/shard_map/dot_general | solution.py:41
  360.3 5.0 %fusion.30 = f32[1024,576]{0,1:T(8,128)S(1)} fusion(bf16[1024,1792]{1,0:T(8,128)(2,1)} %all-gather.6.cloned.1.call-done, bf16[1,4,8192,576]{2,3,1,0:T(8,128)(2,1)} %param.8, s32[]{:T(128)S(6)} %select_n.53), kind=kOutput, calls=%fused_computation.26 | convolution fusion | flops 2113929216 | bytes 8093700 | tf_op jit(solution)/shard_map/dot_general | solution.py:41
  365.3 0.5 collective-permute-start.13
  365.8 4.4 fusion.40
  370.3 4.6 %fusion.42 = f32[1024,576]{0,1:T(8,128)S(1)} fusion(bf16[1024,1536]{1,0:T(8,128)(2,1)} %collective-permute-done.3, bf16[1,4,8192,576]{2,3,1,0:T(8,128)(2,1)} %param.8, s32[]{:T(128)S(6)} %select_n.53), kind=kOutput, calls=%fused_computation.38 | convolution fusion | flops 1811939328 | bytes 7274500 | tf_op jit(solution)/shard_map/dot_general | solution.py:41
  375.0 0.5 copy-done.3
  375.5 0.7 copy-done.4
  376.2 4.9 %add_add_fusion = f32[1024,576]{0,1:T(8,128)S(1)} fusion(f32[1024,576]{0,1:T(8,128)S(1)} %copy-done.3, f32[1024,576]{0,1:T(8,128)S(1)} %fusion.40, f32[1024,576]{0,1:T(8,128)S(1)} %copy-done.4, f32[1024,576]{0,1:T(8,128)S(1)} %fusion.42, f32[1024,576]{0,1:T(8,128)S(1)} %fusion.30, f32[1024,576]{0,1:T(8,128)S(1)} %copy-done.1, f32[1024,576]{0,1:T(8,128)S(1)} %copy-done, ...), kind=kOutput, calls=%fused_computation.21 | convolution fusion | flops 1816657920 | bytes 26148868 | tf_op jit(solution)/shard_map/dot_general | solution.py:41
  381.2 1.1 constant_dynamic-slice_fusion.3
  382.3 0.0 collective-permute-start.8
  382.4 0.9 copy-done.6
  383.2 1.0 add_convert_fusion.3
  384.2 26.6 %collective-permute-start.11 = (bf16[512,576]{0,1:T(8,128)(2,1)}, bf16[512,576]{0,1:T(8,128)(2,1)S(1)}, u32[]{:S(2)}, u32[]{:S(2)}) collective-permute-start(bf16[512,576]{0,1:T(8,128)(2,1)} %add_convert_fusion.3), channel_id=1, source_target_pairs={{0,24},{8,16},{1,25},{9,17},{2,26},{10,18},{3,27},{11,19},{4,28},{... | collective-permute-start | bytes 1769480 | tf_op jit(solution)/shard_map/ppermute | solution.py:82
  410.9 2.3 add_convert_fusion.1
  413.2 4.4 collective-permute-start.17
  417.6 1.0 add_convert_fusion.2
  418.7 2.1 collective-permute-start.14
  420.8 4.0 collective-permute-done.11
  424.8 12.2 %collective-permute-done.17 = bf16[512,576]{0,1:T(8,128)(2,1)S(1)} collective-permute-done((bf16[512,576]{0,1:T(8,128)(2,1)}, bf16[512,576]{0,1:T(8,128)(2,1)S(1)}, u32[]{:S(2)}, u32[]{:S(2)}) %collective-permute-start.17) | collective-permute-done | bytes 589856 | tf_op jit(solution)/shard_map/ppermute | solution.py:82
  437.1 1.9 collective-permute-done.14
  438.9 2.7 fusion.60
  (55 shorter events, 0.2 us)
Async XLA Ops:
  6.5 58.4 %all-gather.12.cloned.1.call-start = ((), (), s32[]{:S(2)}) async-start(), calls=%async_computation.3 | async-start | bytes 2949120 | tf_op jit(solution)/shard_map/all_gather | solution.py:68
  7.3 340.2 %all-gather.10.cloned.1.call-start = ((), (), s32[]{:S(2)}) async-start(), calls=%async_computation.2 | async-start | bytes 4587520 | tf_op jit(solution)/shard_map/all_gather | solution.py:71
  7.3 2.4 collective-permute-start.1
  15.8 49.3 %copy-start.17 = (bf16[256,1792]{1,0:T(8,128)(2,1)}, bf16[256,1792]{1,0:T(8,128)(2,1)S(1)}, u32[]{:S(2)}) copy-start(bf16[256,1792]{1,0:T(8,128)(2,1)S(1)} %fusion.23) | copy-start | bytes 2752516
  15.8 24.7 %collective-permute-start.6 = (bf16[256,1792]{1,0:T(8,128)(2,1)S(1)}, bf16[256,1792]{1,0:T(8,128)(2,1)S(1)}, u32[]{:S(2)}, u32[]{:S(2)}) collective-permute-start(bf16[256,1792]{1,0:T(8,128)(2,1)S(1)} %fusion.23), channel_id=1, source_target_pairs={{0,8},{16,24},{1,9},{17,25},{2,10},{18,26},{3,11},{19,27},{4,12},{... | collective-permute-start | bytes 2752520 | tf_op jit(solution)/shard_map/ppermute | solution.py:67
  40.4 0.9 copy-start.11
  41.4 312.5 %all-gather.8.cloned.1.call-start = ((), (), s32[]{:S(2)}) async-start(), calls=%async_computation.1 | async-start | bytes 4587520 | tf_op jit(solution)/shard_map/all_gather | solution.py:71
  41.4 22.5 %collective-permute-start.4 = (bf16[256,1792]{1,0:T(8,128)(2,1)S(1)}, bf16[256,1792]{1,0:T(8,128)(2,1)S(1)}, u32[]{:S(2)}, u32[]{:S(2)}) collective-permute-start(bf16[256,1792]{1,0:T(8,128)(2,1)S(1)} %fusion.23), channel_id=1, source_target_pairs={{0,16},{8,24},{1,17},{9,25},{2,18},{10,26},{3,19},{11,27},{4,20},{... | collective-permute-start | bytes 2752520 | tf_op jit(solution)/shard_map/ppermute | solution.py:67
  63.9 0.9 copy-start.12
  64.9 295.4 %all-gather.6.cloned.1.call-start = ((), (), s32[]{:S(2)}) async-start(), calls=%async_computation | async-start | bytes 4587520 | tf_op jit(solution)/shard_map/all_gather | solution.py:71
  65.0 28.2 %collective-permute-start = (bf16[1024,1152]{1,0:T(8,128)(2,1)}, bf16[1024,1152]{1,0:T(8,128)(2,1)}, u32[]{:S(2)}, u32[]{:S(2)}) collective-permute-start(bf16[1024,1152]{1,0:T(8,128)(2,1)} %bitcast.60), channel_id=1, source_target_pairs={{0,4},{4,0},{1,5},{5,1},{2,6},{6,2},{3,7},{7,3},{8,12},{12,8},{9,1... | collective-permute-start | bytes 7077896 | tf_op jit(solution)/shard_map/ppermute | solution.py:21
  65.1 23.4 %copy-start.14 = (f32[1,8192]{1,0:T(1,128)S(1)}, f32[1,8192]{1,0:T(1,128)}, u32[]{:S(2)}) copy-start(f32[1,8192]{1,0:T(1,128)} %param.7) | copy-start | bytes 98308
  65.1 28.1 %copy-start.16 = (bf16[1,1024,1152]{2,1,0:T(8,128)(2,1)S(1)}, bf16[1,1024,1152]{2,1,0:T(8,128)(2,1)}, u32[]{:S(2)}) copy-start(bf16[1,1024,1152]{2,1,0:T(8,128)(2,1)} %all-gather.12.cloned.1.call-done) | copy-start | bytes 7077892
  65.1 27.1 %collective-permute-start.2 = (bf16[256,1792]{1,0:T(8,128)(2,1)}, bf16[256,1792]{1,0:T(8,128)(2,1)S(1)}, u32[]{:S(2)}, u32[]{:S(2)}) collective-permute-start(bf16[256,1792]{1,0:T(8,128)(2,1)} %copy-done.17), channel_id=1, source_target_pairs={{0,24},{8,16},{1,25},{9,17},{2,26},{10,18},{3,27},{11,19},{4,28},{... | collective-permute-start | bytes 2752520 | tf_op jit(solution)/shard_map/ppermute | solution.py:67
  84.6 126.7 %collective-permute-start.9 = (bf16[4864,576]{0,1:T(8,128)(2,1)}, bf16[4864,576]{0,1:T(8,128)(2,1)}, u32[]{:S(2)}, u32[]{:S(2)}) collective-permute-start(bf16[4864,576]{0,1:T(8,128)(2,1)} %get-tuple-element.5), channel_id=1, source_target_pairs={{24,0},{16,8},{25,1},{17,9},{26,2},{18,10},{27,3},{19,11},{28,4},{... | collective-permute-start | bytes 16809992 | tf_op jit(solution)/shard_map/ppermute | solution.py:64
  85.9 160.3 %collective-permute-start.15 = (bf16[4864,576]{0,1:T(8,128)(2,1)}, bf16[4864,576]{0,1:T(8,128)(2,1)}, u32[]{:S(2)}, u32[]{:S(2)}) collective-permute-start(bf16[4864,576]{0,1:T(8,128)(2,1)} %get-tuple-element.6), channel_id=1, source_target_pairs={{8,0},{24,16},{9,1},{25,17},{10,2},{26,18},{11,3},{27,19},{12,4},{... | collective-permute-start | bytes 16809992 | tf_op jit(solution)/shard_map/ppermute | solution.py:64
  87.2 243.5 %collective-permute-start.12 = (bf16[4864,576]{0,1:T(8,128)(2,1)}, bf16[4864,576]{0,1:T(8,128)(2,1)}, u32[]{:S(2)}, u32[]{:S(2)}) collective-permute-start(bf16[4864,576]{0,1:T(8,128)(2,1)} %get-tuple-element.7), channel_id=1, source_target_pairs={{16,0},{24,8},{17,1},{25,9},{18,2},{26,10},{19,3},{27,11},{20,4},{... | collective-permute-start | bytes 16809992 | tf_op jit(solution)/shard_map/ppermute | solution.py:64
  92.2 1.0 copy-start.13
  105.9 269.1 %collective-permute-start.7 = (bf16[1024,1536]{1,0:T(8,128)(2,1)}, bf16[1024,1536]{1,0:T(8,128)(2,1)}, u32[]{:S(2)}, u32[]{:S(2)}) collective-permute-start(bf16[1024,1536]{1,0:T(8,128)(2,1)} %maximum_convert_fusion.2), channel_id=1, source_target_pairs={{0,8},{16,24},{1,9},{17,25},{2,10},{18,26},{3,11},{19,27},{4,12},{... | collective-permute-start | bytes 9437192 | tf_op jit(solution)/shard_map/ppermute | solution.py:70
  110.9 254.4 %collective-permute-start.5 = (bf16[1024,1536]{1,0:T(8,128)(2,1)}, bf16[1024,1536]{1,0:T(8,128)(2,1)}, u32[]{:S(2)}, u32[]{:S(2)}) collective-permute-start(bf16[1024,1536]{1,0:T(8,128)(2,1)} %maximum_convert_fusion.2), channel_id=1, source_target_pairs={{0,16},{8,24},{1,17},{9,25},{2,18},{10,26},{3,19},{11,27},{4,20},{... | collective-permute-start | bytes 9437192 | tf_op jit(solution)/shard_map/ppermute | solution.py:70
  211.3 159.0 %collective-permute-start.3 = (bf16[1024,1536]{1,0:T(8,128)(2,1)}, bf16[1024,1536]{1,0:T(8,128)(2,1)}, u32[]{:S(2)}, u32[]{:S(2)}) collective-permute-start(bf16[1024,1536]{1,0:T(8,128)(2,1)} %maximum_convert_fusion.2), channel_id=1, source_target_pairs={{0,24},{8,16},{1,25},{9,17},{2,26},{10,18},{3,27},{11,19},{4,28},{... | collective-permute-start | bytes 9437192 | tf_op jit(solution)/shard_map/ppermute | solution.py:70
  225.2 1.4 copy-start.5
  246.2 136.1 %collective-permute-start.10 = (f32[512,576]{0,1:T(8,128)}, f32[512,576]{0,1:T(8,128)S(1)}, u32[]{:S(2)}, u32[]{:S(2)}) collective-permute-start(f32[512,576]{0,1:T(8,128)} %constant_dynamic-slice_fusion.2), channel_id=1, source_target_pairs={{0,4},{4,0},{1,5},{5,1},{2,6},{6,2},{3,7},{7,3},{8,12},{12,8},{9,1... | collective-permute-start | bytes 3538952 | tf_op jit(solution)/shard_map/ppermute | solution.py:37
  246.2 84.5 %slice-start = ((s8[9961472]{0:T(1024)(128)(4,1)}), s8[4194304]{0:T(1024)(128)(4,1)S(1)}, s32[]{:S(2)}) async-start(s8[9961472]{0:T(1024)(128)(4,1)} %bitcast.64), calls=%async_computation.4 | async-start | bytes 8388608
  246.3 84.5 %slice-start.1 = ((s8[9961472]{0:T(1024)(128)(4,1)}), s8[4194304]{0:T(1024)(128)(4,1)S(1)}, s32[]{:S(2)}) async-start(s8[9961472]{0:T(1024)(128)(4,1)} %bitcast.64), calls=%async_computation.5 | async-start | bytes 8388608
  256.7 1.4 copy-start.7
  259.2 71.5 %slice-start.2 = ((s8[9961472]{0:T(1024)(128)(4,1)}), s8[1572864]{0:T(1024)(128)(4,1)S(1)}, s32[]{:S(2)}) async-start(s8[9961472]{0:T(1024)(128)(4,1)} %bitcast.64), calls=%async_computation.6 | async-start | bytes 3145728
  330.7 80.2 %collective-permute-start.16 = (f32[512,576]{0,1:T(8,128)}, f32[512,576]{0,1:T(8,128)}, u32[]{:S(2)}, u32[]{:S(2)}) collective-permute-start(f32[512,576]{0,1:T(8,128)} %constant_dynamic-slice_fusion), channel_id=1, source_target_pairs={{0,4},{4,0},{1,5},{5,1},{2,6},{6,2},{3,7},{7,3},{8,12},{12,8},{9,1... | collective-permute-start | bytes 3538952 | tf_op jit(solution)/shard_map/ppermute | solution.py:37
  338.9 1.4 copy-start.9
  365.3 52.3 %collective-permute-start.13 = (f32[512,576]{0,1:T(8,128)}, f32[512,576]{0,1:T(8,128)S(1)}, u32[]{:S(2)}, u32[]{:S(2)}) collective-permute-start(f32[512,576]{0,1:T(8,128)} %constant_dynamic-slice_fusion.1), channel_id=1, source_target_pairs={{0,4},{4,0},{1,5},{5,1},{2,6},{6,2},{3,7},{7,3},{8,12},{12,8},{9,1... | collective-permute-start | bytes 3538952 | tf_op jit(solution)/shard_map/ppermute | solution.py:37
  370.3 4.7 %copy-start = (f32[1024,576]{0,1:T(8,128)S(1)}, f32[1024,576]{0,1:T(8,128)}, u32[]{:S(2)}) copy-start(f32[1024,576]{0,1:T(8,128)} %fusion.32) | copy-start | bytes 7077892
  370.3 4.7 %copy-start.1 = (f32[1024,576]{0,1:T(8,128)S(1)}, f32[1024,576]{0,1:T(8,128)}, u32[]{:S(2)}) copy-start(f32[1024,576]{0,1:T(8,128)} %fusion.10) | copy-start | bytes 7077892
  370.3 4.7 %copy-start.2 = (f32[1024,576]{0,1:T(8,128)S(1)}, f32[1024,576]{0,1:T(8,128)}, u32[]{:S(2)}) copy-start(f32[1024,576]{0,1:T(8,128)} %fusion.44) | copy-start | bytes 7077892
  370.3 5.2 %copy-start.3 = (f32[1024,576]{0,1:T(8,128)S(1)}, f32[1024,576]{0,1:T(8,128)}, u32[]{:S(2)}) copy-start(f32[1024,576]{0,1:T(8,128)} %fusion.26) | copy-start | bytes 7077892
  370.3 5.9 %copy-start.4 = (f32[1024,576]{0,1:T(8,128)S(1)}, f32[1024,576]{0,1:T(8,128)}, u32[]{:S(2)}) copy-start(f32[1024,576]{0,1:T(8,128)} %fusion.28) | copy-start | bytes 7077892
  381.1 2.1 copy-start.6
  381.2 29.7 %copy-start.8 = (f32[1024,576]{0,1:T(8,128)S(1)}, f32[1024,576]{0,1:T(8,128)}, u32[]{:S(2)}) copy-start(f32[1024,576]{0,1:T(8,128)} %copy-done.7) | copy-start | bytes 7077892
  382.3 35.3 %copy-start.10 = (f32[1024,576]{0,1:T(8,128)S(1)}, f32[1024,576]{0,1:T(8,128)}, u32[]{:S(2)}) copy-start(f32[1024,576]{0,1:T(8,128)} %copy-done.9) | copy-start | bytes 7077892
  382.3 56.6 %collective-permute-start.8 = (f32[512,576]{0,1:T(8,128)}, f32[512,576]{0,1:T(8,128)}, u32[]{:S(2)}, u32[]{:S(2)}) collective-permute-start(f32[512,576]{0,1:T(8,128)} %constant_dynamic-slice_fusion.3), channel_id=1, source_target_pairs={{0,4},{4,0},{1,5},{5,1},{2,6},{6,2},{3,7},{7,3},{8,12},{12,8},{9,1... | collective-permute-start | bytes 3538952 | tf_op jit(solution)/shard_map/ppermute | solution.py:37
  384.2 36.5 %copy-start.15 = (f32[1,576]{1,0:T(1,128)S(1)}, f32[1,576]{1,0:T(1,128)}, u32[]{:S(2)}) copy-start(f32[1,576]{1,0:T(1,128)} %param.9) | copy-start | bytes 6916
  384.2 40.6 %collective-permute-start.11 = (bf16[512,576]{0,1:T(8,128)(2,1)}, bf16[512,576]{0,1:T(8,128)(2,1)S(1)}, u32[]{:S(2)}, u32[]{:S(2)}) collective-permute-start(bf16[512,576]{0,1:T(8,128)(2,1)} %add_convert_fusion.3), channel_id=1, source_target_pairs={{0,24},{8,16},{1,25},{9,17},{2,26},{10,18},{3,27},{11,19},{4,28},{... | collective-permute-start | bytes 1769480 | tf_op jit(solution)/shard_map/ppermute | solution.py:82
  413.2 23.9 %collective-permute-start.17 = (bf16[512,576]{0,1:T(8,128)(2,1)}, bf16[512,576]{0,1:T(8,128)(2,1)S(1)}, u32[]{:S(2)}, u32[]{:S(2)}) collective-permute-start(bf16[512,576]{0,1:T(8,128)(2,1)} %add_convert_fusion.1), channel_id=1, source_target_pairs={{0,8},{16,24},{1,9},{17,25},{2,10},{18,26},{3,11},{19,27},{4,12},{... | collective-permute-start | bytes 1769480 | tf_op jit(solution)/shard_map/ppermute | solution.py:82
  418.7 20.3 %collective-permute-start.14 = (bf16[512,576]{0,1:T(8,128)(2,1)}, bf16[512,576]{0,1:T(8,128)(2,1)}, u32[]{:S(2)}, u32[]{:S(2)}) collective-permute-start(bf16[512,576]{0,1:T(8,128)(2,1)} %add_convert_fusion.2), channel_id=1, source_target_pairs={{0,16},{8,24},{1,17},{9,25},{2,18},{10,26},{3,19},{11,27},{4,20},{... | collective-permute-start | bytes 1769480 | tf_op jit(solution)/shard_map/ppermute | solution.py:82
Sparse Core Ops, SparseCore 0:
  8.9 53.1 all-gather.11
  63.7 70.9 all-gather.9
  136.2 70.7 all-gather.7
  208.4 70.7 all-gather.5

commit v2 on v1

--- a/solution.py
+++ b/solution.py
@@ -41,13 +41,18 @@
     return jnp.dot(a, b, preferred_element_type=jnp.float32)
 
 
+def after(value, *earlier):
+    return lax.optimization_barrier((value, *earlier))[0]
+
+
 def per_device(sections, shards, inputs, enc_weight, enc_bias, dec_weight, dec_bias):
     encoder, bias, decoders = enc_weight[0], enc_bias[0], dec_weight[0]
     depth = encoder.shape[1]
     me = lax.axis_index("sec")
     rounds = pairs_of(sections)
-    end_z = depth * 7 // 32
-    end_a = depth * 13 // 32
+    end_z = depth * 6 // 32
+    end_a = depth * 12 // 32
+    middle = (end_a + depth) // 2
 
     def encode(rows, low, high):
         hidden = dot(rows, encoder[:, low:high])
@@ -58,31 +63,45 @@
             decoders, (source, low, 0), (1, high - low, decoders.shape[2])
         )[0]
 
-    lent = []
-    for flip, pairs in reversed(rounds):
-        mine = decoder(jnp.minimum(me ^ flip, sections - 1), end_a, depth)
-        lent.append(lax.ppermute(mine, "sec", [(hi, lo) for lo, hi in pairs]))
+    rounds = rounds[::-1]
+    sources = [jnp.minimum(me ^ flip, sections - 1) for flip, _ in rounds]
 
+    def lend(i, low, high, *earlier):
+        mine = after(decoder(sources[i], low, high), *earlier)
+        return lax.ppermute(mine, "sec", [(hi, lo) for lo, hi in rounds[i][1]])
+
+    first = lend(0, end_a, middle)
     rows_z = encode(gather_feat(inputs[0], shards), 0, end_z)
-    near = [lax.ppermute(rows_z, "sec", pairs) for _, pairs in reversed(rounds)]
+    near = [lax.ppermute(rows_z, "sec", pairs) for _, pairs in rounds]
     every = gather_feat(lax.all_gather(inputs[0], "row", axis=0, tiled=True), shards)
+    every = after(every, first)
+    second = lend(0, middle, depth, first)
     feats_a = encode(every, end_z, end_a)
-    direct = [lax.ppermute(feats_a, "sec", pairs) for _, pairs in reversed(rounds)]
+    direct = [lax.ppermute(feats_a, "sec", pairs) for _, pairs in rounds]
     gathered = [lax.all_gather(block, "row", axis=0, tiled=True) for block in near]
+    feats_w = encode(every, end_a, depth)
     feats_z = encode(every, 0, end_z)
-    feats_w = encode(every, end_a, depth)
 
+    def give_back(i, parts):
+        part = scatter_sum_feat(parts, shards)
+        back = lax.ppermute(part.astype(jnp.bfloat16), "sec", rounds[i][1])
+        return back.astype(jnp.float32)
+
+    cut = middle - end_a
+    feats_w = after(feats_w, second)
+    rest = [lend(i, end_a, depth, second) for i in range(1, len(rounds))]
+    returned = give_back(
+        0, dot(feats_w[:, :cut], first) + dot(feats_w[:, cut:], second)
+    )
     total = dot(feats_z, decoder(me, 0, end_z))
     total += dot(feats_a, decoder(me, end_z, end_a))
     total += dot(feats_w, decoder(me, end_a, depth))
-    returned = 0.0
-    for i, (flip, pairs) in enumerate(reversed(rounds)):
-        source = jnp.minimum(me ^ flip, sections - 1)
-        part = scatter_sum_feat(dot(feats_w, lent[i]), shards)
-        back = lax.ppermute(part.astype(jnp.bfloat16), "sec", pairs)
-        returned = returned + back.astype(jnp.float32)
+    for i, source in enumerate(sources):
         total += dot(gathered[i], decoder(source, 0, end_z))
         total += dot(direct[i], decoder(source, end_z, end_a))
+    feats_w = after(feats_w, total)
+    for i in range(1, len(rounds)):
+        returned = returned + give_back(i, dot(feats_w, rest[i - 1]))
     summed = scatter_sum_feat(total, shards) + returned
     return (summed + dec_bias[0]).astype(jnp.bfloat16)[None]
 

time: 449 us -> 415 us (0.924); the launches traced: 448 us -> 409 us
  starting transfers between devices: 71.6 us -> 46.7 us
  waiting for transfers between devices: 180 us -> 165 us
  other arithmetic: 7.03 us -> 13.8 us
  matrix products: 149 us -> 144 us
    ppermute x12 -> x13, starting transfers between devices: 70.2 us -> 45.5 us  [the longest x3 17.1 us: per_device(): near = [lax.ppermute(rows_z, 'sec', pairs) for _, pairs in rounds]]
    ppermute x12 -> x13, waiting for transfers between devices: 178 us -> 163 us  [the longest x4 81 us: lend(): return lax.ppermute(mine, 'sec', [(hi, lo) for lo, hi in rounds[i][1]])]
    select_n x0 -> x1, other arithmetic: none -> 5.53 us  [gather_feat(): jnp.where(first, jnp.concatenate([block, other], axis=1), jnp.concatenate...]
    dot_general x15 -> x16, matrix products: 149 us -> 144 us  [dot(): return jnp.dot(a, b, preferred_element_type=jnp.float32)]
    unnamed x42 -> x38, local copies, waits for them, and re-layouts: 9.26 us -> 5.67 us
    squeeze x1 -> x2, local copies, waits for them, and re-layouts: 12.9 us -> 14.3 us  [decoder(): lax.dynamic_slice(decoders, (source, low, 0), (1, high - low, decoders.sh...]
  transfers between devices with their start and end apart: 22 -> 23, of which waited for: 9 -> 10; matrix products, arithmetic and copies ran while one was open for 38% -> 43% of each run, Pallas kernels for 0% -> 0%
where the time goes in v2:
time: 415 us; the launch traced here: 409 us
  waiting for transfers between devices  165 us (40%)
  matrix products  144 us (35%)
  starting transfers between devices  46.7 us (11%)
  local copies, waits for them, and re-layouts  25.5 us (6%)
  between operations  14 us (3%)
  other arithmetic  13.8 us (3%)
    dot_general x16, matrix products, dot(): return jnp.dot(a, b, preferred_element_type=jnp.float32)  144 us
    ppermute x4, waiting for transfers between devices, lend(): return lax.ppermute(mine, 'sec', [(hi, lo) for lo, hi in rounds[i][1]])  81 us
    ppermute x3, waiting for transfers between devices, per_device(): near = [lax.ppermute(rows_z, 'sec', pairs) for _, pairs in rounds]  40.5 us
    ppermute x3, waiting for transfers between devices, per_device(): direct = [lax.ppermute(feats_a, 'sec', pairs) for _, pairs in rounds]  25.6 us
    ppermute x3, starting transfers between devices, per_device(): near = [lax.ppermute(rows_z, 'sec', pairs) for _, pairs in rounds]  17.1 us
    ppermute x3, waiting for transfers between devices, give_back(): back = lax.ppermute(part.astype(jnp.bfloat16), 'sec', rounds[i][1])  16.4 us
    ppermute x3, starting transfers between devices, per_device(): direct = [lax.ppermute(feats_a, 'sec', pairs) for _, pairs in rounds]  15.9 us
    squeeze x2, local copies, waits for them, and re-layouts, decoder(): lax.dynamic_slice(decoders, (source, low, 0), (1, high - low, decoders.sh...  14.3 us
  transfers between devices with their start and end apart: 23, of which 10 were waited for; matrix products, arithmetic and copies ran while one was open for 43% of the time, Pallas kernels for 0%

profile of v2, /device:TPU:0, one launch (start us, length us, event | category | flops | bytes accessed | tf_op | source)
XLA Modules:
  0.0 409.1 jit_solution(9159686362359554197)
XLA Ops:
  6.5 0.7 all-gather.12.cloned.1.call-update
  7.3 0.5 collective-permute-start.3
  7.8 0.7 slice_reduce_fusion
  8.6 1.1 collective-permute-done.3
  9.7 5.4 %fusion.27 = bf16[256,1536]{1,0:T(8,128)(2,1)S(1)} fusion(bf16[2304,8192]{1,0:T(8,128)(2,1)} %bitcast.65, bf16[256,1152]{1,0:T(8,128)(2,1)S(1)} %collective-permute-done.3, bf16[256,1152]{1,0:T(8,128)(2,1)} %bitcast.63, pred[]{:T(512)S(6)} %eq.4, f32[1536]{0:T(1024)S(1)} %get-tuple-element.18), kind=kOutput, calls=%fused_computation.25 | convolution fusion | flops 1818427392 | bytes 9050113 | tf_op jit(solution)/shard_map/dot_general | solution.py:41
  15.1 4.8 %collective-permute-start.8 = (bf16[256,1536]{1,0:T(8,128)(2,1)S(1)}, bf16[256,1536]{1,0:T(8,128)(2,1)S(1)}, u32[]{:S(2)}, u32[]{:S(2)}) collective-permute-start(bf16[256,1536]{1,0:T(8,128)(2,1)S(1)} %fusion.27), channel_id=1, source_target_pairs={{0,8},{16,24},{1,9},{17,25},{2,10},{18,26},{3,11},{19,27},{4,12},{... | collective-permute-start | bytes 2359304 | tf_op jit(solution)/shard_map/ppermute | solution.py:75
  19.9 17.0 %collective-permute-done.8 = bf16[256,1536]{1,0:T(8,128)(2,1)S(1)} collective-permute-done((bf16[256,1536]{1,0:T(8,128)(2,1)S(1)}, bf16[256,1536]{1,0:T(8,128)(2,1)S(1)}, u32[]{:S(2)}, u32[]{:S(2)}) %collective-permute-start.8) | collective-permute-done | bytes 786464 | tf_op jit(solution)/shard_map/ppermute | solution.py:75
  36.9 0.9 copy-done.12
  37.8 0.0 all-gather.8.cloned.1.call-start
  37.9 3.5 collective-permute-start.6
  41.3 16.2 %collective-permute-done.6 = bf16[256,1536]{1,0:T(8,128)(2,1)S(1)} collective-permute-done((bf16[256,1536]{1,0:T(8,128)(2,1)S(1)}, bf16[256,1536]{1,0:T(8,128)(2,1)S(1)}, u32[]{:S(2)}, u32[]{:S(2)}) %collective-permute-start.6) | collective-permute-done | bytes 786464 | tf_op jit(solution)/shard_map/ppermute | solution.py:75
  57.6 0.9 copy-done.13
  58.5 0.0 all-gather.6.cloned.1.call-start
  58.5 4.7 %dynamic-slice_bitcast_fusion.2 = (bf16[2560,576]{0,1:T(8,128)(2,1)S(1)}, bf16[2560,576]{0,1:T(8,128)(2,1)}) fusion(bf16[1,4,8192,576]{2,3,1,0:T(8,128)(2,1)} %param.8, s32[]{:T(128)S(6)} %select_n.51), kind=kLoop, calls=%fused_computation.21 | loop fusion | bytes 11796484 | tf_op jit(solution)/shard_map/squeeze | solution.py:62
  63.2 1.3 collective-permute-start.1
  64.5 0.1 collective-permute-start
  64.6 8.8 %collective-permute-start.4 = (bf16[256,1536]{1,0:T(8,128)(2,1)}, bf16[256,1536]{1,0:T(8,128)(2,1)}, u32[]{:S(2)}, u32[]{:S(2)}) collective-permute-start(bf16[256,1536]{1,0:T(8,128)(2,1)} %copy-done.15), channel_id=1, source_target_pairs={{0,24},{8,16},{1,25},{9,17},{2,26},{10,18},{3,27},{11,19},{4,28},{... | collective-permute-start | bytes 2359304 | tf_op jit(solution)/shard_map/ppermute | solution.py:75
  73.4 9.6 %dynamic-slice_bitcast_fusion.1 = (bf16[5120,576]{0,1:T(8,128)(2,1)}, bf16[5120,576]{0,1:T(8,128)(2,1)}) fusion(bf16[1,4,8192,576]{2,3,1,0:T(8,128)(2,1)} %param.8, s32[]{:T(128)S(6)} %select_n.55, s32[]{:T(128)S(6)} %select_n.56), kind=kLoop, calls=%fused_computation.14 | loop fusion | bytes 23592968 | tf_op jit(solution)/shard_map/squeeze | solution.py:62
  83.0 7.3 %collective-permute-done.4 = bf16[256,1536]{1,0:T(8,128)(2,1)} collective-permute-done((bf16[256,1536]{1,0:T(8,128)(2,1)}, bf16[256,1536]{1,0:T(8,128)(2,1)}, u32[]{:S(2)}, u32[]{:S(2)}) %collective-permute-start.4) | collective-permute-done | bytes 786464 | tf_op jit(solution)/shard_map/ppermute | solution.py:75
  90.3 41.6 %collective-permute-done.1 = bf16[2560,576]{0,1:T(8,128)(2,1)} collective-permute-done((bf16[2560,576]{0,1:T(8,128)(2,1)}, bf16[2560,576]{0,1:T(8,128)(2,1)}, u32[]{:S(2)}, u32[]{:S(2)}) %collective-permute-start.1) | collective-permute-done | bytes 2949152 | tf_op jit(solution)/shard_map/ppermute | solution.py:71
  132.0 1.3 collective-permute-start.2
  133.3 5.5 %maximum_select_fusion = bf16[1024,2304]{1,0:T(8,128)(2,1)S(1)} fusion(bf16[1024,1152]{1,0:T(8,128)(2,1)} %collective-permute-done, bf16[1024,1152]{1,0:T(8,128)(2,1)} %bitcast.61, pred[]{:T(512)S(6)} %eq.4), kind=kLoop, calls=%fused_computation.20 | loop fusion | flops 21233664 | bytes 9437185 | tf_op jit(solution)/shard_map/jit(_where)/select_n | solution.py:23
  138.8 12.6 %maximum_convert_fusion.1 = bf16[1024,1536]{1,0:T(8,128)(2,1)} fusion(bf16[1024,2304]{1,0:T(8,128)(2,1)S(1)} %maximum_select_fusion, bf16[2304,8192]{1,0:T(8,128)(2,1)} %bitcast.66, f32[1536]{0:T(1024)S(1)} %get-tuple-element.17), kind=kOutput, calls=%fused_computation.5 | convolution fusion | flops 7252475904 | bytes 14948352 | tf_op jit(solution)/shard_map/dot_general | solution.py:41
  151.4 8.4 %collective-permute-start.7 = (bf16[1024,1536]{1,0:T(8,128)(2,1)}, bf16[1024,1536]{1,0:T(8,128)(2,1)}, u32[]{:S(2)}, u32[]{:S(2)}) collective-permute-start(bf16[1024,1536]{1,0:T(8,128)(2,1)} %maximum_convert_fusion.1), channel_id=1, source_target_pairs={{0,16},{8,24},{1,17},{9,25},{2,18},{10,26},{3,19},{11,27},{4,20},{... | collective-permute-start | bytes 9437192 | tf_op jit(solution)/shard_map/ppermute | solution.py:80
  159.8 2.9 collective-permute-start.5
  162.7 4.6 %collective-permute-start.9 = (bf16[1024,1536]{1,0:T(8,128)(2,1)}, bf16[1024,1536]{1,0:T(8,128)(2,1)}, u32[]{:S(2)}, u32[]{:S(2)}) collective-permute-start(bf16[1024,1536]{1,0:T(8,128)(2,1)} %maximum_convert_fusion.1), channel_id=1, source_target_pairs={{0,8},{16,24},{1,9},{17,25},{2,10},{18,26},{3,11},{19,27},{4,12},{... | collective-permute-start | bytes 9437192 | tf_op jit(solution)/shard_map/ppermute | solution.py:80
  167.4 29.1 %maximum_convert_fusion = bf16[1024,5120]{1,0:T(8,128)(2,1)} fusion(bf16[1024,2304]{1,0:T(8,128)(2,1)S(1)} %maximum_select_fusion, bf16[2304,8192]{1,0:T(8,128)(2,1)} %bitcast.67, f32[5120]{0:T(1024)S(1)} %bitcast.64), kind=kOutput, calls=%fused_computation.2 | convolution fusion | flops 24174919680 | bytes 38817792 | tf_op jit(solution)/shard_map/dot_general | solution.py:41
  196.4 2.1 collective-permute-done.2
  198.6 15.7 %fusion.31 = f32[1024,576]{0,1:T(8,128)} fusion(bf16[1024,2304]{1,0:T(8,128)(2,1)} %copy-done.5, bf16[2304,8192]{1,0:T(8,128)(2,1)} %bitcast.68, f32[1536]{0:T(1024)S(1)} %get-tuple-element.18, bf16[1,4,8192,576]{2,3,1,0:T(8,128)(2,1)} %param.8, s32[]{:T(128)S(6)} %select_n.52), kind=kOutput, calls=%fused_computation.26 | convolution fusion | flops 9064415232 | bytes 15931396 | tf_op jit(solution)/shard_map/dot_general | solution.py:41
  214.3 1.3 collective-permute-start.13
  215.6 1.6 collective-permute-start.16
  217.2 12.8 %fusion.10 = f32[1024,576]{0,1:T(8,128)} fusion(bf16[1024,5120]{1,0:T(8,128)(2,1)} %maximum_convert_fusion, bf16[1,4,8192,576]{2,3,1,0:T(8,128)(2,1)} %param.8, s32[]{:T(128)S(6)} %select_n.52), kind=kOutput, calls=%fused_computation.11 | convolution fusion | flops 6039797760 | bytes 18743300 | tf_op jit(solution)/shard_map/dot_general | solution.py:41
  230.0 5.2 %fusion.13 = f32[1024,576]{0,1:T(8,128)S(1)} fusion(bf16[2560,576]{0,1:T(8,128)(2,1)} %collective-permute-done.2, bf16[1024,5120]{1,0:T(8,128)(2,1)S(1)} %bitcast.70), kind=kOutput, calls=%fused_computation.16 | convolution fusion | flops 3019898880 | bytes 10551296 | tf_op jit(solution)/shard_map/dot_general | solution.py:41
  235.3 5.2 %fusion.56 = f32[1024,576]{0,1:T(8,128)S(1)} fusion(f32[1024,576]{0,1:T(8,128)S(1)} %fusion.13, bf16[2560,576]{0,1:T(8,128)(2,1)} %collective-permute-done.1, bf16[1024,5120]{1,0:T(8,128)(2,1)S(1)} %bitcast.70), kind=kOutput, calls=%fused_computation.51 | convolution fusion | flops 3020488704 | bytes 12910592 | tf_op jit(solution)/shard_map/dot_general | solution.py:41
  240.5 1.4 copy-done.6
  242.0 1.1 constant_dynamic-slice_fusion.2
  243.1 5.9 %fusion.45 = f32[1024,576]{0,1:T(8,128)} fusion(bf16[1024,1536]{1,0:T(8,128)(2,1)} %maximum_convert_fusion.1, bf16[1,4,8192,576]{2,3,1,0:T(8,128)(2,1)} %param.8, s32[]{:T(128)S(6)} %select_n.52), kind=kOutput, calls=%fused_computation.40 | convolution fusion | flops 1811939328 | bytes 7274500 | tf_op jit(solution)/shard_map/dot_general | solution.py:41
  249.0 5.9 %fusion.35 = f32[1024,576]{0,1:T(8,128)} fusion(bf16[1024,1536]{1,0:T(8,128)(2,1)} %all-gather.10.cloned.1.call-done, bf16[1,4,8192,576]{2,3,1,0:T(8,128)(2,1)} %param.8, s32[]{:T(128)S(6)} %select_n.56), kind=kOutput, calls=%fused_computation.30 | convolution fusion | flops 1811939328 | bytes 7274500 | tf_op jit(solution)/shard_map/dot_general | solution.py:41
  254.9 5.8 %fusion.39 = f32[1024,576]{0,1:T(8,128)} fusion(bf16[1024,1536]{1,0:T(8,128)(2,1)} %all-gather.8.cloned.1.call-done, bf16[1,4,8192,576]{2,3,1,0:T(8,128)(2,1)} %param.8, s32[]{:T(128)S(6)} %select_n.55), kind=kOutput, calls=%fused_computation.34 | convolution fusion | flops 1811939328 | bytes 7274500 | tf_op jit(solution)/shard_map/dot_general | solution.py:41
  260.7 4.4 %fusion.43 = f32[1024,576]{0,1:T(8,128)S(1)} fusion(bf16[1024,1536]{1,0:T(8,128)(2,1)} %all-gather.6.cloned.1.call-done, bf16[1,4,8192,576]{2,3,1,0:T(8,128)(2,1)} %param.8, s32[]{:T(128)S(6)} %select_n.51), kind=kOutput, calls=%fused_computation.38 | convolution fusion | flops 1811939328 | bytes 7274500 | tf_op jit(solution)/shard_map/dot_general | solution.py:41
  265.1 25.5 %collective-permute-done.7 = bf16[1024,1536]{1,0:T(8,128)(2,1)} collective-permute-done((bf16[1024,1536]{1,0:T(8,128)(2,1)}, bf16[1024,1536]{1,0:T(8,128)(2,1)}, u32[]{:S(2)}, u32[]{:S(2)}) %collective-permute-start.7) | collective-permute-done | bytes 3145760 | tf_op jit(solution)/shard_map/ppermute | solution.py:80
  290.7 4.4 %fusion.37 = f32[1024,576]{0,1:T(8,128)S(1)} fusion(bf16[1024,1536]{1,0:T(8,128)(2,1)} %collective-permute-done.7, bf16[1,4,8192,576]{2,3,1,0:T(8,128)(2,1)} %param.8, s32[]{:T(128)S(6)} %select_n.55), kind=kOutput, calls=%fused_computation.32 | convolution fusion | flops 1811939328 | bytes 7274500 | tf_op jit(solution)/shard_map/dot_general | solution.py:41
  295.2 4.8 %fusion.41 = f32[1024,576]{0,1:T(8,128)S(1)} fusion(bf16[1024,1536]{1,0:T(8,128)(2,1)} %collective-permute-done.5, bf16[1,4,8192,576]{2,3,1,0:T(8,128)(2,1)} %param.8, s32[]{:T(128)S(6)} %select_n.51), kind=kOutput, calls=%fused_computation.36 | convolution fusion | flops 1811939328 | bytes 7274500 | tf_op jit(solution)/shard_map/dot_general | solution.py:41
  300.1 0.3 copy-done.3
  300.4 0.7 copy-done.4
  301.1 4.9 %add_add_fusion = f32[1024,576]{0,1:T(8,128)S(1)} fusion(f32[1024,576]{0,1:T(8,128)S(1)} %copy-done.3, f32[1024,576]{0,1:T(8,128)S(1)} %fusion.37, f32[1024,576]{0,1:T(8,128)S(1)} %copy-done.4, f32[1024,576]{0,1:T(8,128)S(1)} %fusion.41, f32[1024,576]{0,1:T(8,128)S(1)} %fusion.43, f32[1024,576]{0,1:T(8,128)S(1)} %copy-done.1, f32[1024,576]{0,1:T(8,128)S(1)} %copy-done, ...), kind=kOutput, calls=%fused_computation.27 | convolution fusion | flops 1816657920 | bytes 26148868 | tf_op jit(solution)/shard_map/dot_general | solution.py:41
  306.0 37.2 %collective-permute-done.13 = bf16[5120,576]{0,1:T(8,128)(2,1)} collective-permute-done((bf16[5120,576]{0,1:T(8,128)(2,1)}, bf16[5120,576]{0,1:T(8,128)(2,1)}, u32[]{:S(2)}, u32[]{:S(2)}) %collective-permute-start.13) | collective-permute-done | bytes 5898272 | tf_op jit(solution)/shard_map/ppermute | solution.py:71
  343.2 10.7 %fusion.84 = f32[1024,576]{0,1:T(8,128)S(1)} fusion(bf16[1024,5120]{1,0:T(8,128)(2,1)} %maximum_convert_fusion, bf16[5120,576]{0,1:T(8,128)(2,1)} %collective-permute-done.13), kind=kOutput, calls=%fused_computation.86 | convolution fusion | flops 6039797760 | bytes 18743296 | tf_op jit(solution)/shard_map/dot_general | solution.py:41
  353.9 1.2 constant_dynamic-slice_fusion.1
  355.2 10.8 %fusion.85 = f32[1024,576]{0,1:T(8,128)S(1)} fusion(bf16[1024,5120]{1,0:T(8,128)(2,1)} %maximum_convert_fusion, bf16[5120,576]{0,1:T(8,128)(2,1)} %collective-permute-done.16), kind=kOutput, calls=%fused_computation.87 | convolution fusion | flops 6039797760 | bytes 18743296 | tf_op jit(solution)/shard_map/dot_general | solution.py:41
  365.9 1.3 constant_dynamic-slice_fusion
  367.2 0.5 copy-done.10
  367.7 0.5 collective-permute-start.17
  368.2 1.1 constant_dynamic-slice_fusion.3
  369.3 0.9 copy-done.7
  370.3 1.0 add_convert_fusion.3
  371.3 1.4 collective-permute-start.12
  372.8 2.3 add_convert_fusion.2
  375.1 1.4 collective-permute-start.15
  376.5 2.3 add_convert_fusion.1
  378.8 4.2 %collective-permute-start.18 = (bf16[512,576]{0,1:T(8,128)(2,1)}, bf16[512,576]{0,1:T(8,128)(2,1)}, u32[]{:S(2)}, u32[]{:S(2)}) collective-permute-start(bf16[512,576]{0,1:T(8,128)(2,1)} %add_convert_fusion.1), channel_id=1, source_target_pairs={{0,8},{16,24},{1,9},{17,25},{2,10},{18,26},{3,11},{19,27},{4,12},{... | collective-permute-start | bytes 1769480 | tf_op jit(solution)/shard_map/ppermute | solution.py:87
  383.1 3.7 collective-permute-done.12
  386.7 12.7 %collective-permute-done.15 = bf16[512,576]{0,1:T(8,128)(2,1)S(1)} collective-permute-done((bf16[512,576]{0,1:T(8,128)(2,1)}, bf16[512,576]{0,1:T(8,128)(2,1)S(1)}, u32[]{:S(2)}, u32[]{:S(2)}) %collective-permute-start.15) | collective-permute-done | bytes 589856 | tf_op jit(solution)/shard_map/ppermute | solution.py:87
  399.5 2.6 fusion.67
  (56 shorter events, 0.2 us)
Async XLA Ops:
  6.5 58.0 %all-gather.12.cloned.1.call-start = ((), (), s32[]{:S(2)}) async-start(), calls=%async_computation.3 | async-start | bytes 2949120 | tf_op jit(solution)/shard_map/all_gather | solution.py:76
  7.3 241.7 %all-gather.10.cloned.1.call-start = ((), (), s32[]{:S(2)}) async-start(), calls=%async_computation.2 | async-start | bytes 3932160 | tf_op jit(solution)/shard_map/all_gather | solution.py:81
  7.3 2.4 collective-permute-start.3
  15.0 43.5 %copy-start.15 = (bf16[256,1536]{1,0:T(8,128)(2,1)}, bf16[256,1536]{1,0:T(8,128)(2,1)S(1)}, u32[]{:S(2)}) copy-start(bf16[256,1536]{1,0:T(8,128)(2,1)S(1)} %fusion.27) | copy-start | bytes 2359300
  15.1 21.9 %collective-permute-start.8 = (bf16[256,1536]{1,0:T(8,128)(2,1)S(1)}, bf16[256,1536]{1,0:T(8,128)(2,1)S(1)}, u32[]{:S(2)}, u32[]{:S(2)}) collective-permute-start(bf16[256,1536]{1,0:T(8,128)(2,1)S(1)} %fusion.27), channel_id=1, source_target_pairs={{0,8},{16,24},{1,9},{17,25},{2,10},{18,26},{3,11},{19,27},{4,12},{... | collective-permute-start | bytes 2359304 | tf_op jit(solution)/shard_map/ppermute | solution.py:75
  36.9 0.9 copy-start.12
  37.8 217.1 %all-gather.8.cloned.1.call-start = ((), (), s32[]{:S(2)}) async-start(), calls=%async_computation.1 | async-start | bytes 3932160 | tf_op jit(solution)/shard_map/all_gather | solution.py:81
  37.9 19.7 %collective-permute-start.6 = (bf16[256,1536]{1,0:T(8,128)(2,1)S(1)}, bf16[256,1536]{1,0:T(8,128)(2,1)S(1)}, u32[]{:S(2)}, u32[]{:S(2)}) collective-permute-start(bf16[256,1536]{1,0:T(8,128)(2,1)S(1)} %fusion.27), channel_id=1, source_target_pairs={{0,16},{8,24},{1,17},{9,25},{2,18},{10,26},{3,19},{11,27},{4,20},{... | collective-permute-start | bytes 2359304 | tf_op jit(solution)/shard_map/ppermute | solution.py:75
  57.6 0.9 copy-start.13
  58.5 202.2 %all-gather.6.cloned.1.call-start = ((), (), s32[]{:S(2)}) async-start(), calls=%async_computation | async-start | bytes 3932160 | tf_op jit(solution)/shard_map/all_gather | solution.py:81
  63.2 68.7 %collective-permute-start.1 = (bf16[2560,576]{0,1:T(8,128)(2,1)}, bf16[2560,576]{0,1:T(8,128)(2,1)}, u32[]{:S(2)}, u32[]{:S(2)}) collective-permute-start(bf16[2560,576]{0,1:T(8,128)(2,1)} %get-tuple-element.22), channel_id=1, source_target_pairs={{24,0},{16,8},{25,1},{17,9},{26,2},{18,10},{27,3},{19,11},{28,4},{... | collective-permute-start | bytes 8847368 | tf_op jit(solution)/shard_map/ppermute | solution.py:71
  64.5 68.7 %collective-permute-start = (bf16[1024,1152]{1,0:T(8,128)(2,1)}, bf16[1024,1152]{1,0:T(8,128)(2,1)}, u32[]{:S(2)}, u32[]{:S(2)}) collective-permute-start(bf16[1024,1152]{1,0:T(8,128)(2,1)} %bitcast.60), channel_id=1, source_target_pairs={{0,4},{4,0},{1,5},{5,1},{2,6},{6,2},{3,7},{7,3},{8,12},{12,8},{9,1... | collective-permute-start | bytes 7077896 | tf_op jit(solution)/shard_map/ppermute | solution.py:21
  64.6 25.7 %collective-permute-start.4 = (bf16[256,1536]{1,0:T(8,128)(2,1)}, bf16[256,1536]{1,0:T(8,128)(2,1)}, u32[]{:S(2)}, u32[]{:S(2)}) collective-permute-start(bf16[256,1536]{1,0:T(8,128)(2,1)} %copy-done.15), channel_id=1, source_target_pairs={{0,24},{8,16},{1,25},{9,17},{2,26},{10,18},{3,27},{11,19},{4,28},{... | collective-permute-start | bytes 2359304 | tf_op jit(solution)/shard_map/ppermute | solution.py:75
  132.0 66.6 %collective-permute-start.2 = (bf16[2560,576]{0,1:T(8,128)(2,1)S(1)}, bf16[2560,576]{0,1:T(8,128)(2,1)}, u32[]{:S(2)}, u32[]{:S(2)}) collective-permute-start(bf16[2560,576]{0,1:T(8,128)(2,1)S(1)} %get-tuple-element.12), channel_id=1, source_target_pairs={{24,0},{16,8},{25,1},{17,9},{26,2},{18,10},{27,3},{19,11},{28,4},{... | collective-permute-start | bytes 8847368 | tf_op jit(solution)/shard_map/ppermute | solution.py:71
  138.8 28.5 %copy-start.5 = (bf16[1024,2304]{1,0:T(8,128)(2,1)}, bf16[1024,2304]{1,0:T(8,128)(2,1)S(1)}, u32[]{:S(2)}) copy-start(bf16[1024,2304]{1,0:T(8,128)(2,1)S(1)} %maximum_select_fusion) | copy-start | bytes 14155780
  138.8 28.5 %slice-start = ((f32[1,8192]{1,0:T(1,128)}), f32[1,5120]{1,0:T(1,128)S(1)}, s32[]{:S(2)}) async-start(f32[1,8192]{1,0:T(1,128)} %param.7), calls=%async_computation.4 | async-start | bytes 40960 | tf_op jit(solution)/shard_map/slice | solution.py:59
  151.4 139.3 %collective-permute-start.7 = (bf16[1024,1536]{1,0:T(8,128)(2,1)}, bf16[1024,1536]{1,0:T(8,128)(2,1)}, u32[]{:S(2)}, u32[]{:S(2)}) collective-permute-start(bf16[1024,1536]{1,0:T(8,128)(2,1)} %maximum_convert_fusion.1), channel_id=1, source_target_pairs={{0,16},{8,24},{1,17},{9,25},{2,18},{10,26},{3,19},{11,27},{4,20},{... | collective-permute-start | bytes 9437192 | tf_op jit(solution)/shard_map/ppermute | solution.py:80
  159.8 135.4 %collective-permute-start.5 = (bf16[1024,1536]{1,0:T(8,128)(2,1)}, bf16[1024,1536]{1,0:T(8,128)(2,1)}, u32[]{:S(2)}, u32[]{:S(2)}) collective-permute-start(bf16[1024,1536]{1,0:T(8,128)(2,1)} %maximum_convert_fusion.1), channel_id=1, source_target_pairs={{0,24},{8,16},{1,25},{9,17},{2,26},{10,18},{3,27},{11,19},{4,28},{... | collective-permute-start | bytes 9437192 | tf_op jit(solution)/shard_map/ppermute | solution.py:80
  162.7 137.3 %collective-permute-start.9 = (bf16[1024,1536]{1,0:T(8,128)(2,1)}, bf16[1024,1536]{1,0:T(8,128)(2,1)}, u32[]{:S(2)}, u32[]{:S(2)}) collective-permute-start(bf16[1024,1536]{1,0:T(8,128)(2,1)} %maximum_convert_fusion.1), channel_id=1, source_target_pairs={{0,8},{16,24},{1,9},{17,25},{2,10},{18,26},{3,11},{19,27},{4,12},{... | collective-permute-start | bytes 9437192 | tf_op jit(solution)/shard_map/ppermute | solution.py:80
  214.3 128.9 %collective-permute-start.13 = (bf16[5120,576]{0,1:T(8,128)(2,1)}, bf16[5120,576]{0,1:T(8,128)(2,1)}, u32[]{:S(2)}, u32[]{:S(2)}) collective-permute-start(bf16[5120,576]{0,1:T(8,128)(2,1)} %get-tuple-element.15), channel_id=1, source_target_pairs={{16,0},{24,8},{17,1},{25,9},{18,2},{26,10},{19,3},{27,11},{20,4},{... | collective-permute-start | bytes 17694728 | tf_op jit(solution)/shard_map/ppermute | solution.py:71
  215.6 14.4 %slice-start.1 = ((s8[10485760]{0:T(1024)(128)(4,1)}), s8[4194304]{0:T(1024)(128)(4,1)S(1)}, s32[]{:S(2)}) async-start(s8[10485760]{0:T(1024)(128)(4,1)} %bitcast.69), calls=%async_computation.5 | async-start | bytes 8388608
  215.6 14.4 %slice-start.2 = ((s8[10485760]{0:T(1024)(128)(4,1)}), s8[4194304]{0:T(1024)(128)(4,1)S(1)}, s32[]{:S(2)}) async-start(s8[10485760]{0:T(1024)(128)(4,1)} %bitcast.69), calls=%async_computation.6 | async-start | bytes 8388608
  215.6 14.4 %slice-start.3 = ((s8[10485760]{0:T(1024)(128)(4,1)}), s8[2097152]{0:T(1024)(128)(4,1)S(1)}, s32[]{:S(2)}) async-start(s8[10485760]{0:T(1024)(128)(4,1)} %bitcast.69), calls=%async_computation.7 | async-start | bytes 4194304
  215.6 139.5 %collective-permute-start.16 = (bf16[5120,576]{0,1:T(8,128)(2,1)}, bf16[5120,576]{0,1:T(8,128)(2,1)}, u32[]{:S(2)}, u32[]{:S(2)}) collective-permute-start(bf16[5120,576]{0,1:T(8,128)(2,1)} %get-tuple-element.16), channel_id=1, source_target_pairs={{8,0},{24,16},{9,1},{25,17},{10,2},{26,18},{11,3},{27,19},{12,4},{... | collective-permute-start | bytes 17694728 | tf_op jit(solution)/shard_map/ppermute | solution.py:71
  240.5 1.5 copy-start.6
  290.7 78.7 %collective-permute-start.11 = (f32[512,576]{0,1:T(8,128)}, f32[512,576]{0,1:T(8,128)S(1)}, u32[]{:S(2)}, u32[]{:S(2)}) collective-permute-start(f32[512,576]{0,1:T(8,128)} %constant_dynamic-slice_fusion.2), channel_id=1, source_target_pairs={{0,4},{4,0},{1,5},{5,1},{2,6},{6,2},{3,7},{7,3},{8,12},{12,8},{9,1... | collective-permute-start | bytes 3538952 | tf_op jit(solution)/shard_map/ppermute | solution.py:37
  295.1 4.9 %copy-start = (f32[1024,576]{0,1:T(8,128)S(1)}, f32[1024,576]{0,1:T(8,128)}, u32[]{:S(2)}) copy-start(f32[1024,576]{0,1:T(8,128)} %fusion.31) | copy-start | bytes 7077892
  295.1 4.9 %copy-start.1 = (f32[1024,576]{0,1:T(8,128)S(1)}, f32[1024,576]{0,1:T(8,128)}, u32[]{:S(2)}) copy-start(f32[1024,576]{0,1:T(8,128)} %fusion.10) | copy-start | bytes 7077892
  295.2 4.9 %copy-start.2 = (f32[1024,576]{0,1:T(8,128)S(1)}, f32[1024,576]{0,1:T(8,128)}, u32[]{:S(2)}) copy-start(f32[1024,576]{0,1:T(8,128)} %fusion.45) | copy-start | bytes 7077892
  295.2 5.2 %copy-start.3 = (f32[1024,576]{0,1:T(8,128)S(1)}, f32[1024,576]{0,1:T(8,128)}, u32[]{:S(2)}) copy-start(f32[1024,576]{0,1:T(8,128)} %fusion.35) | copy-start | bytes 7077892
  295.2 5.9 %copy-start.4 = (f32[1024,576]{0,1:T(8,128)S(1)}, f32[1024,576]{0,1:T(8,128)}, u32[]{:S(2)}) copy-start(f32[1024,576]{0,1:T(8,128)} %fusion.39) | copy-start | bytes 7077892
  353.9 12.0 %copy-start.8 = (f32[1024,576]{0,1:T(8,128)}, f32[1024,576]{0,1:T(8,128)S(1)}, u32[]{:S(2)}) copy-start(f32[1024,576]{0,1:T(8,128)S(1)} %fusion.84) | copy-start | bytes 7077892
  355.1 17.6 %collective-permute-start.14 = (f32[512,576]{0,1:T(8,128)}, f32[512,576]{0,1:T(8,128)}, u32[]{:S(2)}, u32[]{:S(2)}) collective-permute-start(f32[512,576]{0,1:T(8,128)} %constant_dynamic-slice_fusion.1), channel_id=1, source_target_pairs={{0,4},{4,0},{1,5},{5,1},{2,6},{6,2},{3,7},{7,3},{8,12},{12,8},{9,1... | collective-permute-start | bytes 3538952 | tf_op jit(solution)/shard_map/ppermute | solution.py:37
  365.9 1.8 copy-start.10
  367.7 8.8 %collective-permute-start.17 = (f32[512,576]{0,1:T(8,128)}, f32[512,576]{0,1:T(8,128)}, u32[]{:S(2)}, u32[]{:S(2)}) collective-permute-start(f32[512,576]{0,1:T(8,128)} %constant_dynamic-slice_fusion), channel_id=1, source_target_pairs={{0,4},{4,0},{1,5},{5,1},{2,6},{6,2},{3,7},{7,3},{8,12},{12,8},{9,1... | collective-permute-start | bytes 3538952 | tf_op jit(solution)/shard_map/ppermute | solution.py:37
  368.2 2.1 copy-start.7
  368.2 4.6 %copy-start.9 = (f32[1024,576]{0,1:T(8,128)S(1)}, f32[1024,576]{0,1:T(8,128)}, u32[]{:S(2)}) copy-start(f32[1024,576]{0,1:T(8,128)} %copy-done.8) | copy-start | bytes 7077892
  369.3 7.2 %copy-start.11 = (f32[1024,576]{0,1:T(8,128)S(1)}, f32[1024,576]{0,1:T(8,128)}, u32[]{:S(2)}) copy-start(f32[1024,576]{0,1:T(8,128)} %copy-done.10) | copy-start | bytes 7077892
  369.3 17.4 %collective-permute-start.10 = (f32[512,576]{0,1:T(8,128)}, f32[512,576]{0,1:T(8,128)}, u32[]{:S(2)}, u32[]{:S(2)}) collective-permute-start(f32[512,576]{0,1:T(8,128)} %constant_dynamic-slice_fusion.3), channel_id=1, source_target_pairs={{0,4},{4,0},{1,5},{5,1},{2,6},{6,2},{3,7},{7,3},{8,12},{12,8},{9,1... | collective-permute-start | bytes 3538952 | tf_op jit(solution)/shard_map/ppermute | solution.py:37
  371.3 11.7 %copy-start.14 = (f32[1,576]{1,0:T(1,128)S(1)}, f32[1,576]{1,0:T(1,128)}, u32[]{:S(2)}) copy-start(f32[1,576]{1,0:T(1,128)} %param.9) | copy-start | bytes 6916
  371.3 15.4 %collective-permute-start.12 = (bf16[512,576]{0,1:T(8,128)(2,1)}, bf16[512,576]{0,1:T(8,128)(2,1)S(1)}, u32[]{:S(2)}, u32[]{:S(2)}) collective-permute-start(bf16[512,576]{0,1:T(8,128)(2,1)} %add_convert_fusion.3), channel_id=1, source_target_pairs={{0,24},{8,16},{1,25},{9,17},{2,26},{10,18},{3,27},{11,19},{4,28},{... | collective-permute-start | bytes 1769480 | tf_op jit(solution)/shard_map/ppermute | solution.py:87
  375.1 24.4 %collective-permute-start.15 = (bf16[512,576]{0,1:T(8,128)(2,1)}, bf16[512,576]{0,1:T(8,128)(2,1)S(1)}, u32[]{:S(2)}, u32[]{:S(2)}) collective-permute-start(bf16[512,576]{0,1:T(8,128)(2,1)} %add_convert_fusion.2), channel_id=1, source_target_pairs={{0,16},{8,24},{1,17},{9,25},{2,18},{10,26},{3,19},{11,27},{4,20},{... | collective-permute-start | bytes 1769480 | tf_op jit(solution)/shard_map/ppermute | solution.py:87
  378.8 20.7 %collective-permute-start.18 = (bf16[512,576]{0,1:T(8,128)(2,1)}, bf16[512,576]{0,1:T(8,128)(2,1)}, u32[]{:S(2)}, u32[]{:S(2)}) collective-permute-start(bf16[512,576]{0,1:T(8,128)(2,1)} %add_convert_fusion.1), channel_id=1, source_target_pairs={{0,8},{16,24},{1,9},{17,25},{2,10},{18,26},{3,11},{19,27},{4,12},{... | collective-permute-start | bytes 1769480 | tf_op jit(solution)/shard_map/ppermute | solution.py:87
Sparse Core Ops, SparseCore 0:
  8.9 53.1 all-gather.11
  63.7 62.2 all-gather.9
  127.6 62.1 all-gather.7
  191.2 62.1 all-gather.5
